TPU v7x, 32 devices: a whole 2x2x4 slice. The times are simulated.
32 devices in a mesh: grp: 1, lat: 32 (over z, y, x, core).
Axes of the slice: x: 2, y: 2, z: 4, core: 2. Of those that a mesh axis runs over, the one named last changes fastest.
Arguments:
- grid_field: bfloat16 [192, 1440, 128], P(('grp', 'lat')), may hold values from -6 to 6
- spectral_weight: bfloat16 [4096, 2, 128, 128], P('lat'), may hold values from -0.375 to 0.375
- weight_in: bfloat16 [128, 512], replicated, may hold values from -0.5 to 0.5
- weight_out: bfloat16 [512, 128], replicated, may hold values from -0.25 to 0.25
Outputs:
- layer_out: bfloat16 [192, 1440, 128], P(('grp', 'lat'))
All inputs are finite; a program needn't handle non-finite values.
Results may differ from a plain program's by a relative error of at most 0.008.
Values may be sent and summed in bfloat16 or wider, within the bound.
A program may use at most 64 MiB of HBM per device.

v0:
```python
import math

import jax
import jax.numpy as jnp
from jax import lax
from jax.sharding import PartitionSpec as P

M1 = 64
M2 = 64


def longitude_forward(lon_count):
    modes_lon = jnp.arange(M2, dtype=jnp.int32)
    cells_lon = jnp.arange(lon_count, dtype=jnp.int32)
    angles = (modes_lon[:, None] * cells_lon[None, :] % lon_count).astype(jnp.float32) * (
        2.0 * math.pi / lon_count
    )
    scaled = jnp.stack([jnp.cos(angles), -jnp.sin(angles)], 1) * (1.0 / math.sqrt(lon_count))
    return scaled.astype(jnp.bfloat16)


def longitude_inverse(lon_count):
    modes_lon = jnp.arange(M2, dtype=jnp.int32)
    cells_lon = jnp.arange(lon_count, dtype=jnp.int32)
    angles = (modes_lon[:, None] * cells_lon[None, :] % lon_count).astype(jnp.float32) * (
        2.0 * math.pi / lon_count
    )
    scaled = jnp.stack([jnp.cos(angles), -jnp.sin(angles)], 1) * (1.0 / math.sqrt(M1 * M2))
    return scaled.reshape(2 * M2, lon_count).T.astype(jnp.bfloat16)


def lat_angles(wave_numbers, lat_rows, lat_count):
    product = wave_numbers[:, None] * lat_rows[None, :] % lat_count
    return product.astype(jnp.float32) * (2.0 * math.pi / lat_count)


def wave_of(mode_lat):
    return mode_lat - M1 * (mode_lat >= M1 // 2).astype(jnp.int32)


def per_device(grid_field, spectral_weight, weight_in, weight_out):
    highest = lax.Precision.HIGHEST
    lat_dev = grid_field.shape[0]
    lon_count = grid_field.shape[1]
    channels = grid_field.shape[2]
    lat_count = lax.axis_size("lat") * lat_dev
    local_rows = lax.axis_index("lat") * lat_dev + jnp.arange(lat_dev, dtype=jnp.int32)
    norm_lat = 1.0 / math.sqrt(lat_count)
    forward_table = longitude_forward(lon_count)
    all_waves = wave_of(jnp.arange(M1, dtype=jnp.int32))
    local_angles = lat_angles(all_waves, local_rows, lat_count)
    coeffs = jnp.einsum(
        "mpn,rnc->rmpc", forward_table, grid_field, preferred_element_type=jnp.float32
    ).astype(jnp.bfloat16)
    cos_lat = jnp.cos(local_angles) * norm_lat
    sin_lat = jnp.sin(local_angles) * norm_lat
    real_part = coeffs[:, :, 0].astype(jnp.float32)
    imag_part = coeffs[:, :, 1].astype(jnp.float32)
    real_sum = jnp.einsum("kr,rmc->kmc", cos_lat, real_part, precision=highest) + jnp.einsum(
        "kr,rmc->kmc", sin_lat, imag_part, precision=highest
    )
    imag_sum = jnp.einsum("kr,rmc->kmc", cos_lat, imag_part, precision=highest) - jnp.einsum(
        "kr,rmc->kmc", sin_lat, real_part, precision=highest
    )
    term_all = jnp.stack([real_sum, imag_sum], 2).reshape(M1 * M2, 2, channels)
    spectrum = lax.psum_scatter(term_all, "lat", scatter_dimension=0, tiled=True).astype(
        jnp.bfloat16
    )
    out_real = jnp.einsum(
        "fi,fio->fo", spectrum[:, 0], spectral_weight[:, 0], preferred_element_type=jnp.float32
    ) - jnp.einsum(
        "fi,fio->fo", spectrum[:, 1], spectral_weight[:, 1], preferred_element_type=jnp.float32
    )
    out_imag = jnp.einsum(
        "fi,fio->fo", spectrum[:, 0], spectral_weight[:, 1], preferred_element_type=jnp.float32
    ) + jnp.einsum(
        "fi,fio->fo", spectrum[:, 1], spectral_weight[:, 0], preferred_element_type=jnp.float32
    )
    mixed_modes = jnp.stack([out_real, out_imag], 1).astype(jnp.bfloat16)
    every_mode = lax.all_gather(mixed_modes, "lat", axis=0, tiled=True)
    modes_grid = every_mode.astype(jnp.float32).reshape(M1, M2, 2, channels)
    cos_back = jnp.cos(local_angles)
    sin_back = jnp.sin(local_angles)
    back_real = jnp.einsum(
        "kr,kmc->rmc", cos_back, modes_grid[:, :, 0], precision=highest
    ) - jnp.einsum("kr,kmc->rmc", sin_back, modes_grid[:, :, 1], precision=highest)
    back_imag = jnp.einsum(
        "kr,kmc->rmc", sin_back, modes_grid[:, :, 0], precision=highest
    ) + jnp.einsum("kr,kmc->rmc", cos_back, modes_grid[:, :, 1], precision=highest)
    inverse = (
        jnp.stack([back_real, back_imag], 2).reshape(lat_dev, 2 * M2, channels).astype(jnp.bfloat16)
    )
    spatial = jnp.einsum(
        "nk,rkc->rnc", longitude_inverse(lon_count), inverse, preferred_element_type=jnp.float32
    )
    combined = grid_field.astype(jnp.float32) + spatial
    hidden = jax.nn.gelu(
        jnp.einsum(
            "rnc,ch->rnh",
            combined.astype(jnp.bfloat16),
            weight_in,
            preferred_element_type=jnp.float32,
        )
    ).astype(jnp.bfloat16)
    result = combined + jnp.einsum(
        "rnh,hc->rnc", hidden, weight_out, preferred_element_type=jnp.float32
    )
    return result.astype(jnp.bfloat16)


def solution(mesh):
    in_specs = (P(("grp", "lat"), None, None), P("lat", None, None, None), P(), P())
    out_specs = P(("grp", "lat"), None, None)
    return jax.shard_map(
        per_device, mesh=mesh, in_specs=in_specs, out_specs=out_specs, check_vma=False
    )
```

profile of v0, /device:TPU:0, one launch (start us, length us, event | category | flops | bytes accessed | tf_op | source)
XLA Modules:
  0.0 257.5 jit_solution(14354158552676062516)
XLA Ops:
  6.5 0.0 copy-start
  6.5 0.0 reduce-scatter.2.cloned.1.call-start
  6.5 1.6 sine_negate_fusion
  8.2 2.1 fusion.27
  10.3 1.2 fusion.50
  11.5 1.2 fusion.46
  12.7 1.3 convolution_add_fusion
  14.0 1.2 copy.11
  15.2 1.2 convolution_subtract_fusion
  16.4 1.2 copy.14
  17.6 2.2 pad_maximum_fusion
  19.8 0.0 reduce-scatter.2.cloned.1.call-update
  19.9 0.2 all-gather.2.cloned.1.call-start
  20.1 143.4 %reduce-scatter.2.cloned.1.call-done = f32[128,2,128]{2,0,1:T(8,128)} async-done(((f32[4096,2,128]{2,0,1:T(8,128)}), f32[128,2,128]{2,0,1:T(8,128)}) %reduce-scatter.2.cloned.1.call-update) | async-done | bytes 131088 | tf_op jit(solution)/shard_map/reduce_scatter | solution.py:66
  163.5 0.9 convert_element_type.66
  164.5 3.4 %fusion.12 = f32[128,1,128]{2,1,0:T(1,128)S(1)} fusion(bf16[128,2,128,128]{3,2,1,0:T(8,128)(2,1)} %param.5, bf16[128,128,1]{1,0,2:T(8,128)(2,1)S(1)} %get-tuple-element.9), kind=kOutput, calls=%fused_computation.16 | convolution fusion | flops 4194304 | bytes 4292608 | tf_op jit(solution)/shard_map/fi,fio->fo/dot_general | solution.py:76
  167.9 3.4 %fusion.10 = f32[128,1,128]{2,1,0:T(1,128)S(1)} fusion(bf16[128,2,128,128]{3,2,1,0:T(8,128)(2,1)} %param.5, bf16[128,128,1]{1,0,2:T(8,128)(2,1)S(1)} %get-tuple-element.9), kind=kOutput, calls=%fused_computation.14 | convolution fusion | flops 4194304 | bytes 4292608 | tf_op jit(solution)/shard_map/fi,fio->fo/dot_general | solution.py:71
  171.3 3.4 %fusion.8 = f32[128,1,128]{2,1,0:T(1,128)S(1)} fusion(bf16[128,2,128,128]{3,2,1,0:T(8,128)(2,1)} %param.5, bf16[128,128,1]{1,0,2:T(8,128)(2,1)S(1)} %get-tuple-element.10), kind=kOutput, calls=%fused_computation.12 | convolution fusion | flops 4194304 | bytes 4292608 | tf_op jit(solution)/shard_map/fi,fio->fo/dot_general | solution.py:74
  174.7 3.4 %fusion.14 = f32[128,1,128]{2,1,0:T(1,128)S(1)} fusion(bf16[128,2,128,128]{3,2,1,0:T(8,128)(2,1)} %param.5, bf16[128,128,1]{1,0,2:T(8,128)(2,1)S(1)} %get-tuple-element.10), kind=kOutput, calls=%fused_computation.18 | convolution fusion | flops 4194304 | bytes 4292608 | tf_op jit(solution)/shard_map/fi,fio->fo/dot_general | solution.py:69
  178.1 0.6 pad_maximum_fusion.3
  178.8 0.0 all-gather.2.cloned.1.call-update
  178.8 0.1 multiply_convert_fusion
  178.8 0.4 copy.18
  179.2 0.3 convert_element_type.69
  179.5 51.8 %all-gather.2.cloned.1.call-done = bf16[4096,2,128]{2,0,1:T(8,128)(2,1)} async-done(((bf16[128,2,128]{2,0,1:T(8,128)(2,1)}), bf16[4096,2,128]{2,0,1:T(8,128)(2,1)}) %all-gather.2.cloned.1.call-update) | async-done | bytes 2097168 | tf_op jit(solution)/shard_map/all_gather | solution.py:80
  231.4 1.7 fusion.165
  233.1 0.0 copy-start.1
  233.1 1.0 fusion.34
  234.1 1.0 fusion.35
  235.1 1.0 fusion.33
  236.2 1.0 fusion.32
  237.2 0.0 copy-start.2
  237.2 0.1 pad_maximum_fusion.2
  237.3 0.2 copy.17
  237.5 0.0 copy-done.1
  237.5 2.8 %bitcast_add_fusion = f32[6,1440,128]{2,1,0:T(8,128)} fusion(bf16[6,1440,128]{2,1,0:T(8,128)(2,1)S(1)} %copy-done.1, bf16[6,128,128]{2,1,0:T(8,128)(2,1)S(1)} %bitcast.98, bf16[128,1440]{1,0:T(8,128)(2,1)S(1)} %convert_element_type.69), kind=kOutput, calls=%fused_computation.9 | convolution fusion | flops 285327360 | bytes 7200768 | tf_op jit(solution)/shard_map/nk,rkc->rnc/dot_general | solution.py:93
  240.3 0.0 copy-done
  240.3 0.0 copy-done.2
  240.3 10.3 %add_convert_fusion = bf16[6,1440,128]{2,1,0:T(8,128)(2,1)} fusion(f32[6,1440,128]{2,1,0:T(8,128)} %bitcast_add_fusion, bf16[512,128]{1,0:T(8,128)(2,1)S(1)} %copy-done, bf16[128,512]{1,0:T(8,128)(2,1)S(1)} %copy-done.2), kind=kOutput, calls=%fused_computation.10 | convolution fusion | flops 2308055040 | bytes 6897664 | tf_op jit(solution)/shard_map/rnh,hc->rnc/dot_general | solution.py:105
  (6 shorter events, 0.1 us)
Async XLA Ops:
  6.5 233.8 %copy-start = (bf16[512,128]{1,0:T(8,128)(2,1)S(1)}, bf16[512,128]{1,0:T(8,128)(2,1)}, u32[]{:S(2)}) copy-start(bf16[512,128]{1,0:T(8,128)(2,1)} %param.7) | copy-start | bytes 393220
  6.5 157.0 %reduce-scatter.2.cloned.1.call-start = ((), (), s32[]{:S(2)}) async-start(), calls=%async_computation.1 | async-start | bytes 4325376 | tf_op jit(solution)/shard_map/reduce_scatter | solution.py:66
  19.9 211.5 %all-gather.2.cloned.1.call-start = ((), (), s32[]{:S(2)}) async-start(), calls=%async_computation.2 | async-start | bytes 2162688 | tf_op jit(solution)/shard_map/all_gather | solution.py:80
  233.1 4.4 %copy-start.1 = (bf16[6,1440,128]{2,1,0:T(8,128)(2,1)S(1)}, bf16[6,1440,128]{2,1,0:T(8,128)(2,1)}, u32[]{:S(2)}) copy-start(bf16[6,1440,128]{2,1,0:T(8,128)(2,1)} %param.4) | copy-start | bytes 6635524
  237.2 3.1 %copy-start.2 = (bf16[128,512]{1,0:T(8,128)(2,1)S(1)}, bf16[128,512]{1,0:T(8,128)(2,1)}, u32[]{:S(2)}) copy-start(bf16[128,512]{1,0:T(8,128)(2,1)} %param.6) | copy-start | bytes 393220
Sparse Core Ops, SparseCore 0:
  20.0 143.5 reduce-scatter.1
  178.9 52.4 all-gather.1
where the time goes:
time: 258 us; the launch traced here: 257 us
  waiting for transfers between devices  195 us (76%)
  matrix products  37.7 us (15%)
  between operations  13.6 us (5%)
  other arithmetic  5.56 us (2%)
  local copies, waits for them, and re-layouts  5.06 us (2%)
    reduce_scatter x1, waiting for transfers between devices, per_device(): lax.psum_scatter(term_all, 'lat', scatter_dimension=0, tiled=True)  143 us
    all_gather x1, waiting for transfers between devices, per_device(): every_mode = lax.all_gather(mixed_modes, 'lat', axis=0, tiled=True)  51.8 us
    dot_general x1, matrix products, per_device(): jnp.einsum('rnh,hc->rnc', hidden, weight_out, preferred_element_type=jnp....  10.3 us
  transfers between devices with their start and end apart: 2, of which 2 were waited for; matrix products, arithmetic and copies ran while one was open for 0% of the time, Pallas kernels for 0%

commit v1 on v0

v1 whole, which is shorter than its diff:
```python
import functools
import math

import jax
import jax.numpy as jnp
import ml_dtypes
import numpy as np
from jax import lax
from jax.experimental import pallas as pl
from jax.experimental.pallas import tpu as pltpu
from jax.sharding import PartitionSpec as P

M1 = 64
M2 = 64
BF = jnp.bfloat16
MESH = pl.DeviceIdType.MESH


def np_bf16(values):
    return np.asarray(values, np.float32).astype(ml_dtypes.bfloat16)


def longitude_tables(lon_count):
    modes_lon = np.arange(M2)
    cells_lon = np.arange(lon_count)
    angles = (modes_lon[:, None] * cells_lon[None, :] % lon_count) * (2.0 * math.pi / lon_count)
    both = np.stack([np.cos(angles), -np.sin(angles)], 1).reshape(2 * M2, lon_count)
    forward = np_bf16(both / math.sqrt(lon_count))
    inverse = np_bf16((both / math.sqrt(M1 * M2)).T)
    return forward, inverse


def wave_of(mode_lat):
    return mode_lat - M1 * (mode_lat >= M1 // 2).astype(np.int32)


def latitude_tables(shards, lat_dev):
    lat_count = shards * lat_dev
    mb = M2 // shards
    waves = wave_of(np.arange(M1))
    theta = (waves[:, None] * np.arange(lat_count)[None, :] % lat_count) * (
        2.0 * math.pi / lat_count
    )
    cos, sin = np.cos(theta), np.sin(theta)
    eye = np.eye(mb)
    turn = np.stack([np.stack([cos, sin], 2), np.stack([-sin, cos], 2)], 1)
    forward = np.einsum("kprq,mn->kmprnq", turn, eye) / math.sqrt(lat_count)
    forward = forward.reshape(M1 * mb * 2, lat_count * mb * 2)
    turn = np.stack([np.stack([cos, -sin], 2), np.stack([sin, cos], 2)], 1)
    turn = np.einsum("kprq->rpkq", turn)
    inverse = np.einsum("rpkq,mn->rmpknq", turn, eye)
    inverse = inverse.reshape(lat_count * mb * 2, M1 * mb * 2)
    return np_bf16(forward), np_bf16(inverse)


def swap_table(rows):
    table = np.zeros((rows, rows))
    even = np.arange(0, rows, 2)
    table[even, even + 1] = -1.0
    table[even + 1, even] = 1.0
    return np_bf16(table)


def regroup_table(shards):
    table = np.zeros((shards * 8, shards * 8))
    for a in range(2):
        for s in range(shards):
            for q in range(4):
                table[(a * shards + s) * 4 + q, (s * 2 + a) * 4 + q] = 1.0
    return np_bf16(table)


def send_all(n, me, src, dst, send_sem, recv_sem):
    own = pltpu.make_async_copy(src.at[me], dst.at[me], recv_sem)
    own.start()

    def step(s, carry):
        dest = lax.rem(me + s, n)
        pltpu.make_async_remote_copy(
            src_ref=src.at[dest],
            dst_ref=dst.at[me],
            send_sem=send_sem,
            recv_sem=recv_sem,
            device_id={"lat": dest},
            device_id_type=MESH,
        ).start()
        return carry

    lax.fori_loop(1, n, step, 0)


def wait_recv(dst, recv_sem):
    pltpu.make_async_copy(dst, dst, recv_sem).wait()


def wait_send(n, src, send_sem):
    part = src.at[pl.ds(0, n - 1)]
    pltpu.make_async_copy(part, part, send_sem).wait()


def spectral_kernel(
    n,
    grid_hbm,
    weight_hbm,
    table_hbm,
    fwd_hbm,
    inv_hbm,
    swap_hbm,
    regroup_hbm,
    out_ref,
    grid_v,
    weight_v,
    table_v,
    fwd_v,
    inv_v,
    swap_v,
    regroup_v,
    send1,
    recv1,
    send2,
    recv2,
    send3,
    recv3,
    send4,
    recv4,
    load_sem,
    send_sem,
    recv_sem,
):
    me = lax.axis_index("lat")
    lat_dev = grid_v.shape[0]
    channels = grid_v.shape[2]
    loads = [
        pltpu.make_async_copy(a, b, load_sem.at[i])
        for i, (a, b) in enumerate(
            [
                (table_hbm, table_v),
                (grid_hbm, grid_v),
                (fwd_hbm, fwd_v),
                (swap_hbm, swap_v),
                (weight_hbm, weight_v),
                (inv_hbm, inv_v),
                (regroup_hbm, regroup_v),
            ]
        )
    ]
    for load in loads:
        load.start()
    barrier = pltpu.get_barrier_semaphore()

    def greet(s, carry):
        pl.semaphore_signal(
            barrier, inc=1, device_id={"lat": lax.rem(me + s, n)}, device_id_type=MESH
        )
        return carry

    lax.fori_loop(1, n, greet, 0)
    loads[0].wait()
    loads[1].wait()
    half = 2 * M2
    low = lax.broadcasted_iota(jnp.int32, (n // 2, 8, channels), 1) < 4
    for t in range(lat_dev // 2):
        pair = jnp.concatenate([grid_v[2 * t], grid_v[2 * t + 1]], axis=1)
        got = jnp.dot(table_v[...], pair, preferred_element_type=jnp.float32)
        shape = (n // 2, 8, channels)
        a0 = got[:half, :channels].reshape(shape)
        a1 = got[:half, channels:].reshape(shape)
        b0 = got[half:, :channels].reshape(shape)
        b1 = got[half:, channels:].reshape(shape)
        even = jnp.where(low, a0, b1)
        odd = jnp.where(low, b0, a1)
        send1[:, t] = jnp.stack([even, odd], 1).reshape(n, 8, channels).astype(BF)
    pl.semaphore_wait(barrier, n - 1)
    send_all(n, me, send1, recv1, send_sem.at[0], recv_sem.at[0])
    loads[2].wait()
    wait_recv(recv1, recv_sem.at[0])
    block = recv1[...].astype(jnp.float32).reshape(-1, channels).astype(BF)
    spectrum = jnp.dot(fwd_v[...], block, preferred_element_type=jnp.float32)
    send2[...] = spectrum.reshape(n, 8, channels).astype(BF)
    send_all(n, me, send2, recv2, send_sem.at[1], recv_sem.at[1])
    loads[3].wait()
    loads[4].wait()
    wait_recv(recv2, recv_sem.at[1])
    plain = recv2[...].astype(jnp.float32).reshape(n * 8, channels).astype(BF)
    turned = jnp.dot(swap_v[...], plain, preferred_element_type=jnp.float32).astype(BF)
    both = jnp.concatenate([plain, turned], axis=1).astype(jnp.float32)
    mb = M2 // n
    row = lax.broadcasted_iota(jnp.int32, (8, channels), 0)
    for s in range(n):
        lhs = both[8 * s : 8 * s + 8].astype(BF)
        acc = None
        for q in range(4):
            f = (q // mb) * M2 + s * mb + q % mb
            part = jnp.dot(lhs, weight_v[f], preferred_element_type=jnp.float32)
            acc = part if acc is None else jnp.where(row < 2 * q, acc, part)
        send3[s] = acc.astype(BF)
    send_all(n, me, send3, recv3, send_sem.at[2], recv_sem.at[2])
    loads[5].wait()
    loads[6].wait()
    wait_recv(recv3, recv_sem.at[2])
    block = recv3[...].astype(jnp.float32).reshape(-1, channels).astype(BF)
    back = jnp.dot(inv_v[...], block, preferred_element_type=jnp.float32)
    send4[...] = back.reshape(send4.shape).astype(BF)
    send_all(n, me, send4, recv4, send_sem.at[3], recv_sem.at[3])
    wait_recv(recv4, recv_sem.at[3])
    for t in range(lat_dev // 2):
        block = recv4[:, t].astype(jnp.float32).reshape(-1, channels).astype(BF)
        rows = jnp.dot(regroup_v[...], block, preferred_element_type=jnp.float32).astype(BF)
        out_ref[t] = jnp.concatenate([rows[:half], rows[half:]], axis=1)
    wait_send(n, send1, send_sem.at[0])
    wait_send(n, send2, send_sem.at[1])
    wait_send(n, send3, send_sem.at[2])
    wait_send(n, send4, send_sem.at[3])


def spectral(n, grid_field, spectral_weight):
    lat_dev, lon_count, channels = grid_field.shape
    forward, _ = longitude_tables(lon_count)
    swapped = forward.reshape(-1, 2, 4, lon_count)[:, ::-1].reshape(2 * M2, lon_count)
    table = np.concatenate([forward, swapped], 0)
    fwd, inv = latitude_tables(n, lat_dev)
    swap = swap_table(n * 8)
    regroup = regroup_table(n)
    weight = spectral_weight.reshape(spectral_weight.shape[0], 2 * channels, channels)
    tiles = lat_dev // 2
    operands = [
        grid_field, weight, jnp.asarray(table), jnp.asarray(fwd), jnp.asarray(inv),
        jnp.asarray(swap), jnp.asarray(regroup),
    ]
    big = pltpu.VMEM((n, tiles, 8, channels), BF)
    small = pltpu.VMEM((n, 8, channels), BF)
    return pl.pallas_call(
        functools.partial(spectral_kernel, n),
        out_shape=jax.ShapeDtypeStruct((tiles, 2 * M2, 2 * channels), BF),
        in_specs=[pl.BlockSpec(memory_space=pl.ANY)] * len(operands),
        out_specs=pl.BlockSpec(memory_space=pltpu.VMEM),
        scratch_shapes=[pltpu.VMEM(x.shape, BF) for x in operands]
        + [big, big, small, small, small, small, big, big]
        + [
            pltpu.SemaphoreType.DMA((len(operands),)),
            pltpu.SemaphoreType.DMA((4,)),
            pltpu.SemaphoreType.DMA((4,)),
        ],
        compiler_params=pltpu.CompilerParams(
            collective_id=0, has_side_effects=True, vmem_limit_bytes=40 * 1024 * 1024
        ),
    )(*operands)


GELU_IN = math.sqrt(2.0 / math.pi)


def gelu(x):
    inner = x * (x * x * (0.044715 * GELU_IN) + GELU_IN)
    half = 0.5 * x
    return half + half * jnp.tanh(inner)


def finish_kernel(sub, grid_ref, inv_ref, table_ref, win_ref, wout_ref, out_ref):
    rows, channels = grid_ref.shape[1:]
    for lo in range(0, rows, sub):
        spatial = jnp.dot(
            table_ref[lo : lo + sub], inv_ref[0], preferred_element_type=jnp.float32
        )
        for a in range(2):
            cells = grid_ref[a, lo : lo + sub].astype(jnp.float32)
            combined = cells + spatial[:, a * channels : (a + 1) * channels]
            pre = jnp.dot(
                combined.astype(BF), win_ref[...], preferred_element_type=jnp.float32
            )
            hidden = gelu(pre.astype(BF))
            result = combined + jnp.dot(
                hidden, wout_ref[...], preferred_element_type=jnp.float32
            )
            out_ref[a, lo : lo + sub] = result.astype(BF)


def finish(grid_field, inverse, weight_in, weight_out):
    lat_dev, lon_count, channels = grid_field.shape
    _, table = longitude_tables(lon_count)
    block = lon_count // 2
    sub = block // 3
    return pl.pallas_call(
        functools.partial(finish_kernel, sub),
        grid=(lon_count // block, lat_dev // 2),
        out_shape=jax.ShapeDtypeStruct(grid_field.shape, BF),
        in_specs=[
            pl.BlockSpec((2, block, channels), lambda i, t: (t, i, 0)),
            pl.BlockSpec((1, 2 * M2, 2 * channels), lambda i, t: (t, 0, 0)),
            pl.BlockSpec((block, 2 * M2), lambda i, t: (i, 0)),
            pl.BlockSpec(weight_in.shape, lambda i, t: (0, 0)),
            pl.BlockSpec(weight_out.shape, lambda i, t: (0, 0)),
        ],
        out_specs=pl.BlockSpec((2, block, channels), lambda i, t: (t, i, 0)),
        compiler_params=pltpu.CompilerParams(vmem_limit_bytes=40 * 1024 * 1024),
    )(grid_field, inverse, jnp.asarray(table), weight_in, weight_out)


def spectral_wide(n, grid_field, spectral_weight):
    highest = lax.Precision.HIGHEST
    lat_dev, lon_count, channels = grid_field.shape
    lat_count = n * lat_dev
    rows = lax.axis_index("lat") * lat_dev + jnp.arange(lat_dev, dtype=jnp.int32)
    waves = jnp.asarray(wave_of(np.arange(M1)), jnp.int32)
    angles = (waves[:, None] * rows[None, :] % lat_count).astype(jnp.float32) * (
        2.0 * math.pi / lat_count
    )
    forward = jnp.asarray(longitude_tables(lon_count)[0]).reshape(M2, 2, lon_count)
    coeffs = jnp.einsum(
        "mpn,rnc->rmpc", forward, grid_field, preferred_element_type=jnp.float32
    ).astype(BF)
    cos, sin = jnp.cos(angles), jnp.sin(angles)
    turn = jnp.stack([jnp.stack([cos, sin], -1), jnp.stack([-sin, cos], -1)], 1)
    terms = jnp.einsum(
        "kprq,rmqc->kmpc",
        turn / math.sqrt(lat_count),
        coeffs.astype(jnp.float32),
        precision=highest,
    ).reshape(M1 * M2, 2, channels)
    spectrum = lax.psum_scatter(terms, "lat", scatter_dimension=0, tiled=True).astype(BF)
    product = functools.partial(
        jnp.einsum, "fi,fio->fo", preferred_element_type=jnp.float32
    )
    re, im = spectrum[:, 0], spectrum[:, 1]
    w_re, w_im = spectral_weight[:, 0], spectral_weight[:, 1]
    mixed = jnp.stack(
        [product(re, w_re) - product(im, w_im), product(re, w_im) + product(im, w_re)], 1
    ).astype(BF)
    modes = lax.all_gather(mixed, "lat", axis=0, tiled=True)
    modes = modes.astype(jnp.float32).reshape(M1, M2, 2, channels)
    turn = jnp.stack([jnp.stack([cos, -sin], -1), jnp.stack([sin, cos], -1)], 1)
    back = jnp.einsum("kprq,kmqc->rmpc", turn, modes, precision=highest)
    back = back.reshape(lat_dev // 2, 2, 2 * M2, channels).astype(BF)
    return back.transpose(0, 2, 1, 3).reshape(lat_dev // 2, 2 * M2, 2 * channels)


def per_device(grid_field, spectral_weight, weight_in, weight_out):
    n = lax.axis_size("lat")
    blocks_fit = M2 % n == 0 and M1 % n == 0 and (M1 // n) * (M2 // n) == 4
    step = spectral if blocks_fit else spectral_wide
    inverse = step(n, grid_field, spectral_weight)
    return finish(grid_field, inverse, weight_in, weight_out)


def solution(mesh):
    in_specs = (P(("grp", "lat"), None, None), P("lat", None, None, None), P(), P())
    out_specs = P(("grp", "lat"), None, None)
    return jax.shard_map(
        per_device, mesh=mesh, in_specs=in_specs, out_specs=out_specs, check_vma=False
    )
```

time: 258 us -> 54.8 us (0.21)
  waiting for transfers between devices: 195 us -> 0 us
  Pallas kernels: 0 us -> 44.4 us
  matrix products: 37.7 us -> 0 us
  between operations: 13.6 us -> 0.04 us
  other arithmetic: 5.56 us -> 0 us
  local copies, waits for them, and re-layouts: 5.06 us -> 9.95 us
    reduce_scatter x1 -> x0, waiting for transfers between devices: 143 us -> none  [per_device(): lax.psum_scatter(term_all, 'lat', scatter_dimension=0, tiled=True)]
    all_gather x1 -> x0, waiting for transfers between devices: 51.8 us -> none  [per_device(): every_mode = lax.all_gather(mixed_modes, 'lat', axis=0, tiled=True)]
    pallas_call x0 -> x2, Pallas kernels: none -> 44.4 us  [the longest x1 32.1 us: spectral(): pl.pallas_call(functools.partial(spectral_kernel, n), out_shape=jax.Shape...]
    dot_general x15 -> x0, matrix products: 37.7 us -> none  [the longest x1 10.3 us: per_device(): jnp.einsum('rnh,hc->rnc', hidden, weight_out, preferred_element_type=jnp....]
    unnamed x6 -> x20, local copies, waits for them, and re-layouts: 0.02 us -> 9.95 us
    another operation x5 -> x0, other arithmetic: 2.95 us -> none  [the longest x1 2.22 us: per_device(): term_all = jnp.stack([real_sum, imag_sum], 2).reshape(M1 * M2, 2, channels)]
  transfers between devices with their start and end apart: 2 -> 0, of which waited for: 2 -> 0; matrix products, arithmetic and copies ran while one was open for 0% -> 0% of each run, Pallas kernels for 0% -> 0%
where the time goes in v1:
time: 54.8 us; the launch traced here: 54.4 us
  Pallas kernels  44.4 us (81%)
  local copies, waits for them, and re-layouts  9.95 us (18%)
    pallas_call x1, Pallas kernels, spectral(): pl.pallas_call(functools.partial(spectral_kernel, n), out_shape=jax.Shape...  32.1 us
    pallas_call x1, Pallas kernels, finish(): pl.pallas_call(functools.partial(finish_kernel, sub), grid=(lon_count //...  12.4 us
    unnamed x20, local copies, waits for them, and re-layouts  9.95 us

profile of v1, /device:TPU:0, one launch (start us, length us, event | category | flops | bytes accessed | tf_op | source)
XLA Modules:
  0.0 54.4 jit_solution(16980843150963871921)
XLA Ops:
  0.0 0.0 copy-start
  0.0 1.6 %copy-done = bf16[6,1440,128]{2,1,0:T(8,128)(2,1)S(1)} copy-done((bf16[6,1440,128]{2,1,0:T(8,128)(2,1)S(1)}, bf16[6,1440,128]{2,1,0:T(8,128)(2,1)}, u32[]{:S(2)}) %copy-start) | copy-done | bytes 2211864
  1.6 0.0 copy-start.1
  1.6 3.4 %copy-done.1 = bf16[128,2,128,128]{3,2,1,0:T(8,128)(2,1)S(1)} copy-done((bf16[128,2,128,128]{3,2,1,0:T(8,128)(2,1)S(1)}, bf16[128,2,128,128]{3,2,1,0:T(8,128)(2,1)}, u32[]{:S(2)}) %copy-start.1) | copy-done | bytes 8388632
  5.0 0.0 copy-start.2
  5.0 1.1 %copy-done.2 = bf16[256,1440]{1,0:T(8,128)(2,1)S(1)} copy-done((bf16[256,1440]{1,0:T(8,128)(2,1)S(1)}, bf16[256,1440]{1,0:T(8,128)(2,1)}, u32[]{:S(2)}) %copy-start.2) | copy-done | bytes 737304
  6.1 0.0 copy-start.3
  6.1 1.0 %copy-done.3 = bf16[768,256]{1,0:T(8,128)(2,1)S(1)} copy-done((bf16[768,256]{1,0:T(8,128)(2,1)S(1)}, bf16[768,256]{1,0:T(8,128)(2,1)}, u32[]{:S(2)}) %copy-start.3) | copy-done | bytes 393240
  7.1 0.0 copy-start.4
  7.1 1.0 %copy-done.4 = bf16[256,768]{1,0:T(8,128)(2,1)S(1)} copy-done((bf16[256,768]{1,0:T(8,128)(2,1)S(1)}, bf16[256,768]{1,0:T(8,128)(2,1)}, u32[]{:S(2)}) %copy-start.4) | copy-done | bytes 393240
  8.1 0.0 copy-start.6
  8.1 0.9 %copy-done.6 = bf16[256,256]{1,0:T(8,128)(2,1)S(1)} copy-done((bf16[256,256]{1,0:T(8,128)(2,1)S(1)}, bf16[256,256]{1,0:T(8,128)(2,1)}, u32[]{:S(2)}) %copy-start.6) | copy-done | bytes 131096
  9.0 0.0 copy-start.7
  9.0 0.9 %copy-done.7 = bf16[256,256]{1,0:T(8,128)(2,1)S(1)} copy-done((bf16[256,256]{1,0:T(8,128)(2,1)S(1)}, bf16[256,256]{1,0:T(8,128)(2,1)}, u32[]{:S(2)}) %copy-start.7) | copy-done | bytes 131096
  9.9 0.0 copy-start.5
  9.9 0.0 copy-start.8
  9.9 0.0 copy-start.9
  9.9 32.1 %shard_map.100.inv_ref = bf16[3,128,256]{2,1,0:T(8,128)(2,1)S(1)} custom-call(bf16[6,1440,128]{2,1,0:T(8,128)(2,1)S(1)} %copy-done, bf16[128,256,128]{2,1,0:T(8,128)(2,1)S(1)} %bitcast.1, bf16[256,1440]{1,0:T(8,128)(2,1)S(1)} %copy-done.2, bf16[256,768]{1,0:T(8,128)(2,1)S(1)} %copy-done.4, bf16[768,256]{1,0:T(8,128)(2,1)S(1)} %copy-done.3, ...), custom_call_target="tpu_custom_call" | custom-call | tf_op jit(solution)/shard_map/pallas_call | solution.py:232
  42.0 0.0 copy-done.5
  42.0 0.0 copy-done.8
  42.1 0.0 copy-done.9
  42.1 12.4 %shard_map.101 = bf16[6,1440,128]{2,1,0:T(8,128)(2,1)} custom-call(bf16[6,1440,128]{2,1,0:T(8,128)(2,1)S(1)} %copy-done, bf16[3,128,256]{2,1,0:T(8,128)(2,1)S(1)} %shard_map.100.inv_ref, bf16[1440,128]{1,0:T(8,128)(2,1)S(1)} %copy-done.5, bf16[128,512]{1,0:T(8,128)(2,1)S(1)} %copy-done.8, bf16[512,128]{1,0:T(8,128)(2,1)S(1)} %copy-done.9), custom_call_target="tpu_custom_call" | custom-call | tf_op jit(solution)/shard_map/pallas_call | solution.py:283
Async XLA Ops:
  0.0 1.6 %copy-start = (bf16[6,1440,128]{2,1,0:T(8,128)(2,1)S(1)}, bf16[6,1440,128]{2,1,0:T(8,128)(2,1)}, u32[]{:S(2)}) copy-start(bf16[6,1440,128]{2,1,0:T(8,128)(2,1)} %grid_ref.1) | copy-start | bytes 6635524
  1.6 3.4 %copy-start.1 = (bf16[128,2,128,128]{3,2,1,0:T(8,128)(2,1)S(1)}, bf16[128,2,128,128]{3,2,1,0:T(8,128)(2,1)}, u32[]{:S(2)}) copy-start(bf16[128,2,128,128]{3,2,1,0:T(8,128)(2,1)} %param.11) | copy-start | bytes 25165828
  5.0 1.1 %copy-start.2 = (bf16[256,1440]{1,0:T(8,128)(2,1)S(1)}, bf16[256,1440]{1,0:T(8,128)(2,1)}, u32[]{:S(2)}) copy-start(bf16[256,1440]{1,0:T(8,128)(2,1)} %constant.12.clone.table_hbm) | copy-start | bytes 2211844
  6.1 1.0 %copy-start.3 = (bf16[768,256]{1,0:T(8,128)(2,1)S(1)}, bf16[768,256]{1,0:T(8,128)(2,1)}, u32[]{:S(2)}) copy-start(bf16[768,256]{1,0:T(8,128)(2,1)} %constant.14.clone.inv_hbm) | copy-start | bytes 1179652
  7.1 1.0 %copy-start.4 = (bf16[256,768]{1,0:T(8,128)(2,1)S(1)}, bf16[256,768]{1,0:T(8,128)(2,1)}, u32[]{:S(2)}) copy-start(bf16[256,768]{1,0:T(8,128)(2,1)} %constant.13.clone.fwd_hbm) | copy-start | bytes 1179652
  8.1 0.9 %copy-start.6 = (bf16[256,256]{1,0:T(8,128)(2,1)S(1)}, bf16[256,256]{1,0:T(8,128)(2,1)}, u32[]{:S(2)}) copy-start(bf16[256,256]{1,0:T(8,128)(2,1)} %constant.16.clone.regroup_hbm) | copy-start | bytes 393220
  9.0 0.9 %copy-start.7 = (bf16[256,256]{1,0:T(8,128)(2,1)S(1)}, bf16[256,256]{1,0:T(8,128)(2,1)}, u32[]{:S(2)}) copy-start(bf16[256,256]{1,0:T(8,128)(2,1)} %constant.15.clone.swap_hbm) | copy-start | bytes 393220
  9.9 32.1 %copy-start.5 = (bf16[1440,128]{1,0:T(8,128)(2,1)S(1)}, bf16[1440,128]{1,0:T(8,128)(2,1)}, u32[]{:S(2)}) copy-start(bf16[1440,128]{1,0:T(8,128)(2,1)} %constant.17.clone.table_ref) | copy-start | bytes 1105924
  9.9 32.1 %copy-start.8 = (bf16[128,512]{1,0:T(8,128)(2,1)S(1)}, bf16[128,512]{1,0:T(8,128)(2,1)}, u32[]{:S(2)}) copy-start(bf16[128,512]{1,0:T(8,128)(2,1)} %win_ref.1) | copy-start | bytes 393220
  9.9 32.1 %copy-start.9 = (bf16[512,128]{1,0:T(8,128)(2,1)S(1)}, bf16[512,128]{1,0:T(8,128)(2,1)}, u32[]{:S(2)}) copy-start(bf16[512,128]{1,0:T(8,128)(2,1)} %wout_ref.1) | copy-start | bytes 393220

commit v2 on v1

--- a/solution.py
+++ b/solution.py
@@ -144,8 +144,8 @@
             ]
         )
     ]
-    for load in loads:
-        load.start()
+    loads[0].start()
+    loads[1].start()
     barrier = pltpu.get_barrier_semaphore()
 
     def greet(s, carry):
@@ -157,6 +157,8 @@
     lax.fori_loop(1, n, greet, 0)
     loads[0].wait()
     loads[1].wait()
+    for load in loads[2:]:
+        load.start()
     half = 2 * M2
     low = lax.broadcasted_iota(jnp.int32, (n // 2, 8, channels), 1) < 4
     for t in range(lat_dev // 2):
@@ -232,7 +234,7 @@
     return pl.pallas_call(
         functools.partial(spectral_kernel, n),
         out_shape=jax.ShapeDtypeStruct((tiles, 2 * M2, 2 * channels), BF),
-        in_specs=[pl.BlockSpec(memory_space=pl.ANY)] * len(operands),
+        in_specs=[pl.BlockSpec(memory_space=pltpu.HBM)] * len(operands),
         out_specs=pl.BlockSpec(memory_space=pltpu.VMEM),
         scratch_shapes=[pltpu.VMEM(x.shape, BF) for x in operands]
         + [big, big, small, small, small, small, big, big]
@@ -242,7 +244,7 @@
             pltpu.SemaphoreType.DMA((4,)),
         ],
         compiler_params=pltpu.CompilerParams(
-            collective_id=0, has_side_effects=True, vmem_limit_bytes=40 * 1024 * 1024
+            collective_id=0, has_side_effects=True, vmem_limit_bytes=56 * 1056 * 1056
         ),
     )(*operands)
 
@@ -278,8 +280,8 @@
 def finish(grid_field, inverse, weight_in, weight_out):
     lat_dev, lon_count, channels = grid_field.shape
     _, table = longitude_tables(lon_count)
-    block = lon_count // 2
-    sub = block // 3
+    block = lon_count
+    sub = block
     return pl.pallas_call(
         functools.partial(finish_kernel, sub),
         grid=(lon_count // block, lat_dev // 2),
@@ -292,7 +294,7 @@
             pl.BlockSpec(weight_out.shape, lambda i, t: (0, 0)),
         ],
         out_specs=pl.BlockSpec((2, block, channels), lambda i, t: (t, i, 0)),
-        compiler_params=pltpu.CompilerParams(vmem_limit_bytes=40 * 1024 * 1024),
+        compiler_params=pltpu.CompilerParams(vmem_limit_bytes=32 * 1024 * 1024),
     )(grid_field, inverse, jnp.asarray(table), weight_in, weight_out)
 
 

time: 54.8 us -> 39 us (0.71)
  local copies, waits for them, and re-layouts: 9.95 us -> 0.93 us
  Pallas kernels: 44.4 us -> 37.9 us
    unnamed x20 -> x10, local copies, waits for them, and re-layouts: 9.95 us -> 0.93 us
    pallas_call x1, Pallas kernels: 12.4 us -> 6.75 us  [finish(): pl.pallas_call(functools.partial(finish_kernel, sub), grid=(lon_count //...]
    pallas_call x1, Pallas kernels: 32.1 us -> 31.2 us  [spectral(): pl.pallas_call(functools.partial(spectral_kernel, n), out_shape=jax.Shape...]
where the time goes in v2:
time: 39 us; the launch traced here: 38.9 us
  Pallas kernels  37.9 us (97%)
  local copies, waits for them, and re-layouts  0.93 us (2%)
    pallas_call x1, Pallas kernels, spectral(): pl.pallas_call(functools.partial(spectral_kernel, n), out_shape=jax.Shape...  31.2 us
    pallas_call x1, Pallas kernels, finish(): pl.pallas_call(functools.partial(finish_kernel, sub), grid=(lon_count //...  6.75 us
    unnamed x10, local copies, waits for them, and re-layouts  0.93 us

profile of v2, /device:TPU:0, one launch (start us, length us, event | category | flops | bytes accessed | tf_op | source)
XLA Modules:
  0.0 38.9 jit_solution(14329260060061406563)
XLA Ops:
  0.0 0.0 copy-start
  0.0 0.0 copy-start.2
  0.0 0.0 copy-start.3
  0.0 0.0 copy-start.4
  0.0 31.2 %shard_map.100.inv_ref = bf16[3,128,256]{2,1,0:T(8,128)(2,1)} custom-call(bf16[6,1440,128]{2,1,0:T(8,128)(2,1)} %grid_ref.1, bf16[128,256,128]{2,1,0:T(8,128)(2,1)} %bitcast.1, bf16[256,1440]{1,0:T(8,128)(2,1)} %constant.12.clone.table_hbm, bf16[256,768]{1,0:T(8,128)(2,1)} %constant.13.clone.fwd_hbm, bf16[768,256]{1,0:T(8,128)(2,1)} %constant.14.clone.inv_hbm, ...), custom_call_target="tpu_custom_call" | custom-call | tf_op jit(solution)/shard_map/pallas_call | solution.py:234
  31.2 0.0 copy-done
  31.2 0.0 copy-done.2
  31.2 0.0 copy-done.3
  31.2 0.0 copy-done.4
  31.2 0.0 copy-start.1
  31.2 0.9 %copy-done.1 = bf16[3,128,256]{2,1,0:T(8,128)(2,1)S(1)} copy-done((bf16[3,128,256]{2,1,0:T(8,128)(2,1)S(1)}, bf16[3,128,256]{2,1,0:T(8,128)(2,1)}, u32[]{:S(2)}) %copy-start.1) | copy-done | bytes 196632
  32.1 6.7 %shard_map.101 = bf16[6,1440,128]{2,1,0:T(8,128)(2,1)} custom-call(bf16[6,1440,128]{2,1,0:T(8,128)(2,1)S(1)} %copy-done, bf16[3,128,256]{2,1,0:T(8,128)(2,1)S(1)} %copy-done.1, bf16[1440,128]{1,0:T(8,128)(2,1)S(1)} %copy-done.2, bf16[128,512]{1,0:T(8,128)(2,1)S(1)} %copy-done.3, bf16[512,128]{1,0:T(8,128)(2,1)S(1)} %copy-done.4), custom_call_target="tpu_custom_call" | custom-call | tf_op jit(solution)/shard_map/pallas_call | solution.py:285
Async XLA Ops:
  0.0 31.2 %copy-start = (bf16[6,1440,128]{2,1,0:T(8,128)(2,1)S(1)}, bf16[6,1440,128]{2,1,0:T(8,128)(2,1)}, u32[]{:S(2)}) copy-start(bf16[6,1440,128]{2,1,0:T(8,128)(2,1)} %grid_ref.1) | copy-start | bytes 6635524
  0.0 31.2 %copy-start.2 = (bf16[1440,128]{1,0:T(8,128)(2,1)S(1)}, bf16[1440,128]{1,0:T(8,128)(2,1)}, u32[]{:S(2)}) copy-start(bf16[1440,128]{1,0:T(8,128)(2,1)} %constant.17.clone.table_ref) | copy-start | bytes 1105924
  0.0 31.2 %copy-start.3 = (bf16[128,512]{1,0:T(8,128)(2,1)S(1)}, bf16[128,512]{1,0:T(8,128)(2,1)}, u32[]{:S(2)}) copy-start(bf16[128,512]{1,0:T(8,128)(2,1)} %win_ref.1) | copy-start | bytes 393220
  0.0 31.2 %copy-start.4 = (bf16[512,128]{1,0:T(8,128)(2,1)S(1)}, bf16[512,128]{1,0:T(8,128)(2,1)}, u32[]{:S(2)}) copy-start(bf16[512,128]{1,0:T(8,128)(2,1)} %wout_ref.1) | copy-start | bytes 393220
  31.2 0.9 %copy-start.1 = (bf16[3,128,256]{2,1,0:T(8,128)(2,1)S(1)}, bf16[3,128,256]{2,1,0:T(8,128)(2,1)}, u32[]{:S(2)}) copy-start(bf16[3,128,256]{2,1,0:T(8,128)(2,1)} %shard_map.100.inv_ref) | copy-start | bytes 589828

commit v3 on v2

--- a/solution.py
+++ b/solution.py
@@ -244,7 +244,7 @@
             pltpu.SemaphoreType.DMA((4,)),
         ],
         compiler_params=pltpu.CompilerParams(
-            collective_id=0, has_side_effects=True, vmem_limit_bytes=56 * 1056 * 1056
+            collective_id=0, has_side_effects=True, vmem_limit_bytes=58 * 1024 * 1024
         ),
     )(*operands)
 
@@ -258,14 +258,14 @@
     return half + half * jnp.tanh(inner)
 
 
-def finish_kernel(sub, grid_ref, inv_ref, table_ref, win_ref, wout_ref, out_ref):
+def finish_kernel(grid_ref, inv_ref, table_ref, win_ref, wout_ref, out_hbm, held, sems):
     rows, channels = grid_ref.shape[1:]
-    for lo in range(0, rows, sub):
-        spatial = jnp.dot(
-            table_ref[lo : lo + sub], inv_ref[0], preferred_element_type=jnp.float32
-        )
+    copies = []
+    for t in range(grid_ref.shape[0] // 2):
+        spatial = jnp.dot(table_ref[...], inv_ref[t], preferred_element_type=jnp.float32)
         for a in range(2):
-            cells = grid_ref[a, lo : lo + sub].astype(jnp.float32)
+            r = 2 * t + a
+            cells = grid_ref[r].astype(jnp.float32)
             combined = cells + spatial[:, a * channels : (a + 1) * channels]
             pre = jnp.dot(
                 combined.astype(BF), win_ref[...], preferred_element_type=jnp.float32
@@ -274,26 +274,26 @@
             result = combined + jnp.dot(
                 hidden, wout_ref[...], preferred_element_type=jnp.float32
             )
-            out_ref[a, lo : lo + sub] = result.astype(BF)
+            held[r] = result.astype(BF)
+            copy = pltpu.make_async_copy(held.at[r], out_hbm.at[r], sems.at[r])
+            copy.start()
+            copies.append(copy)
+    for copy in copies:
+        copy.wait()
 
 
 def finish(grid_field, inverse, weight_in, weight_out):
-    lat_dev, lon_count, channels = grid_field.shape
+    lat_dev, lon_count, _ = grid_field.shape
     _, table = longitude_tables(lon_count)
-    block = lon_count
-    sub = block
     return pl.pallas_call(
-        functools.partial(finish_kernel, sub),
-        grid=(lon_count // block, lat_dev // 2),
+        finish_kernel,
         out_shape=jax.ShapeDtypeStruct(grid_field.shape, BF),
-        in_specs=[
-            pl.BlockSpec((2, block, channels), lambda i, t: (t, i, 0)),
-            pl.BlockSpec((1, 2 * M2, 2 * channels), lambda i, t: (t, 0, 0)),
-            pl.BlockSpec((block, 2 * M2), lambda i, t: (i, 0)),
-            pl.BlockSpec(weight_in.shape, lambda i, t: (0, 0)),
-            pl.BlockSpec(weight_out.shape, lambda i, t: (0, 0)),
+        in_specs=[pl.BlockSpec(memory_space=pltpu.VMEM)] * 5,
+        out_specs=pl.BlockSpec(memory_space=pltpu.HBM),
+        scratch_shapes=[
+            pltpu.VMEM(grid_field.shape, BF),
+            pltpu.SemaphoreType.DMA((lat_dev,)),
         ],
-        out_specs=pl.BlockSpec((2, block, channels), lambda i, t: (t, i, 0)),
         compiler_params=pltpu.CompilerParams(vmem_limit_bytes=32 * 1024 * 1024),
     )(grid_field, inverse, jnp.asarray(table), weight_in, weight_out)
 

time: 39 us -> 38.6 us (0.990)
  Pallas kernels: 37.9 us -> 37.5 us
    pallas_call x1, Pallas kernels: 6.75 us -> 6.34 us  [finish(): pl.pallas_call(finish_kernel, out_shape=jax.ShapeDtypeStruct(grid_field.s...]
where the time goes in v3:
time: 38.6 us; the launch traced here: 38.5 us
  Pallas kernels  37.5 us (97%)
  local copies, waits for them, and re-layouts  0.93 us (2%)
    pallas_call x1, Pallas kernels, spectral(): pl.pallas_call(functools.partial(spectral_kernel, n), out_shape=jax.Shape...  31.2 us
    pallas_call x1, Pallas kernels, finish(): pl.pallas_call(finish_kernel, out_shape=jax.ShapeDtypeStruct(grid_field.s...  6.34 us
    unnamed x10, local copies, waits for them, and re-layouts  0.93 us

profile of v3, /device:TPU:0, one launch (start us, length us, event | category | flops | bytes accessed | tf_op | source)
XLA Modules:
  0.0 38.5 jit_solution(5211131737946750734)
XLA Ops:
  0.0 0.0 copy-start
  0.0 0.0 copy-start.2
  0.0 0.0 copy-start.3
  0.0 0.0 copy-start.4
  0.0 31.2 %shard_map.100.inv_ref = bf16[3,128,256]{2,1,0:T(8,128)(2,1)} custom-call(bf16[6,1440,128]{2,1,0:T(8,128)(2,1)} %grid_ref.1, bf16[128,256,128]{2,1,0:T(8,128)(2,1)} %bitcast.1, bf16[256,1440]{1,0:T(8,128)(2,1)} %constant.12.clone.table_hbm, bf16[256,768]{1,0:T(8,128)(2,1)} %constant.13.clone.fwd_hbm, bf16[768,256]{1,0:T(8,128)(2,1)} %constant.14.clone.inv_hbm, ...), custom_call_target="tpu_custom_call" | custom-call | tf_op jit(solution)/shard_map/pallas_call | solution.py:234
  31.2 0.0 copy-done
  31.2 0.0 copy-done.2
  31.2 0.0 copy-done.3
  31.2 0.0 copy-done.4
  31.2 0.0 copy-start.1
  31.2 0.9 %copy-done.1 = bf16[3,128,256]{2,1,0:T(8,128)(2,1)S(1)} copy-done((bf16[3,128,256]{2,1,0:T(8,128)(2,1)S(1)}, bf16[3,128,256]{2,1,0:T(8,128)(2,1)}, u32[]{:S(2)}) %copy-start.1) | copy-done | bytes 196632
  32.1 6.3 %shard_map.101 = bf16[6,1440,128]{2,1,0:T(8,128)(2,1)} custom-call(bf16[6,1440,128]{2,1,0:T(8,128)(2,1)S(1)} %copy-done, bf16[3,128,256]{2,1,0:T(8,128)(2,1)S(1)} %copy-done.1, bf16[1440,128]{1,0:T(8,128)(2,1)S(1)} %copy-done.2, bf16[128,512]{1,0:T(8,128)(2,1)S(1)} %copy-done.3, bf16[512,128]{1,0:T(8,128)(2,1)S(1)} %copy-done.4), custom_call_target="tpu_custom_call" | custom-call | tf_op jit(solution)/shard_map/pallas_call | solution.py:288
Async XLA Ops:
  0.0 31.2 %copy-start = (bf16[6,1440,128]{2,1,0:T(8,128)(2,1)S(1)}, bf16[6,1440,128]{2,1,0:T(8,128)(2,1)}, u32[]{:S(2)}) copy-start(bf16[6,1440,128]{2,1,0:T(8,128)(2,1)} %grid_ref.1) | copy-start | bytes 6635524
  0.0 31.2 %copy-start.2 = (bf16[1440,128]{1,0:T(8,128)(2,1)S(1)}, bf16[1440,128]{1,0:T(8,128)(2,1)}, u32[]{:S(2)}) copy-start(bf16[1440,128]{1,0:T(8,128)(2,1)} %constant.17.clone.table_ref) | copy-start | bytes 1105924
  0.0 31.2 %copy-start.3 = (bf16[128,512]{1,0:T(8,128)(2,1)S(1)}, bf16[128,512]{1,0:T(8,128)(2,1)}, u32[]{:S(2)}) copy-start(bf16[128,512]{1,0:T(8,128)(2,1)} %win_ref.1) | copy-start | bytes 393220
  0.0 31.2 %copy-start.4 = (bf16[512,128]{1,0:T(8,128)(2,1)S(1)}, bf16[512,128]{1,0:T(8,128)(2,1)}, u32[]{:S(2)}) copy-start(bf16[512,128]{1,0:T(8,128)(2,1)} %wout_ref.1) | copy-start | bytes 393220
  31.2 0.9 %copy-start.1 = (bf16[3,128,256]{2,1,0:T(8,128)(2,1)S(1)}, bf16[3,128,256]{2,1,0:T(8,128)(2,1)}, u32[]{:S(2)}) copy-start(bf16[3,128,256]{2,1,0:T(8,128)(2,1)} %shard_map.100.inv_ref) | copy-start | bytes 589828
